TPU v7x, 512 devices: a whole 4x4x16 slice. The times are simulated.
512 devices in a mesh: ctx: 32 (over z_lo, y), tp: 8 (over z_hi, x), dp: 2 (over core).
Axes of the slice: x: 4, y: 4, z: 16 (z_hi: 2, z_lo: 8; z = z_hi * 8 + z_lo), core: 2. Of those that a mesh axis runs over, the one named last changes fastest.
Arguments:
- vis_qkv: bfloat16 [32768, 3, 1280], P(('dp', 'ctx'), None, 'tp'), parts along dimension 0, may hold values from -60 to 60
- vis_resid: bfloat16 [32768, 1280], P(('dp', 'ctx'), 'tp'), parts along dimension 0, may hold values from -1.796875 to 1.796875
- vis_out_w: bfloat16 [1280, 1280], P(None, 'tp'), may hold values from -0.15625 to 0.15625
- merge_gain: float32 [1280], P('tp'), may hold values from 0.5 to 1.5
- merge_bias: float32 [1280], P('tp'), may hold values from -3 to 3
- vis_kv_w: bfloat16 [4, 1280, 2048], P(None, 'tp'), may hold values from -0.078125 to 0.078125
- frame_host: int32 [64], P('dp'), parts along dimension 0, may hold values from 0 to 31, as said below
- vis_pos: int32 [64], P('dp'), parts along dimension 0, may hold values from 0 to 8064, as said below
- doc_ids: int32 [16384], P('dp'), parts along dimension 0, may hold values from 0 to 3, as said below
- text_kv: bfloat16 [16384, 8, 2, 128], P(('dp', 'ctx'), 'tp'), parts along dimension 0, may hold values from -4 to 4
- queries: bfloat16 [16384, 4096], P(('dp', 'ctx'), 'tp'), parts along dimension 0, may hold values from -50 to 50
Outputs:
- attended: bfloat16 [16384, 4096], P(('dp', 'ctx'), 'tp'), parts along dimension 0
There are 2 independent parts, one for each index of `dp`. A program takes and returns all parts, laid end to end along the dimension named above; an argument that names none is the same for every part. Nothing has to cross between parts.
Inputs may be any that keep to these rules, and one draw needn't show every extreme that they name: `vis_pos`: frame starts are multiples of 128 and increase with the frame; some block of 256 positions holds only frames. `frame_host`: each frame is encoded on the ctx device that holds its positions or on the device 32 / 2 indices away along ctx; every device encodes exactly 1 frame. `doc_ids`: never falls along the sequence.
All inputs are finite; a program needn't handle non-finite values.
Results may differ from a plain program's by a relative error of at most 0.0085.
Values may be sent and summed in bfloat16 or wider, within the bound.
A program may use at most 64 MiB of HBM per device.

v0:
```python
import math

import jax
import jax.numpy as jnp
from jax import lax
from jax.sharding import PartitionSpec as P

VD = 1280
VH = 16
HD = 128
H = 32
KVH = 8
FT = 128


NEGATIVE = -1e30


def passed_along(block, axis, distance):
    devices = range(lax.axis_size(axis))
    route = [((i - distance) % len(devices), i) for i in devices]
    return lax.ppermute(block, axis, route)


def frame_tables(frame_host, vis_pos, device, per_device, frames_dev):
    count = frame_host.shape[0]
    frame_ids = jnp.arange(count, dtype=jnp.int32)
    earlier = frame_ids[None, :] < frame_ids[:, None]
    same_host = frame_host[:, None] == frame_host[None, :]
    target = vis_pos // per_device
    moving = target != frame_host
    host_rank = jnp.sum(jnp.where(same_host & earlier, 1, 0), axis=1)
    send_rank = jnp.sum(jnp.where(same_host & earlier & moving[None, :], 1, 0), axis=1)
    slot_ids = jnp.arange(frames_dev, dtype=jnp.int32)
    leaving = (frame_host == device) & moving
    send_hit = jnp.any(
        leaving[None, None, :]
        & (send_rank[None, None, :] == slot_ids[:, None, None])
        & (host_rank[None, None, :] == slot_ids[None, :, None]),
        axis=2,
    )
    sending = jnp.where(send_hit, 1.0, 0.0).astype(jnp.bfloat16)
    slot_count = per_device // FT
    arriving = target == device
    local_slot = (vis_pos - device * per_device) // FT
    source = jnp.where(moving, frames_dev + send_rank, host_rank)
    slot_range = jnp.arange(slot_count, dtype=jnp.int32)
    source_range = jnp.arange(2 * frames_dev, dtype=jnp.int32)
    at_slot = arriving[None, :] & (local_slot[None, :] == slot_range[:, None])
    place_hit = jnp.any(
        at_slot[:, None, :] & (source[None, None, :] == source_range[None, :, None]), axis=2
    )
    placing = jnp.where(place_hit, 1.0, 0.0).astype(jnp.bfloat16)
    filled = jnp.any(at_slot, axis=1)
    return (sending, placing, filled)


def shards(
    vis_qkv,
    vis_resid,
    vis_out_w,
    merge_gain,
    merge_bias,
    vis_kv_w,
    frame_host,
    vis_pos,
    doc_ids,
    text_kv,
    queries,
):
    device = lax.axis_index("ctx")
    peers = lax.axis_size("ctx")
    per_device = queries.shape[0]
    patches = vis_qkv.shape[0]
    frames_dev = patches // (4 * FT)
    local_width = vis_qkv.shape[2]
    head_dim = VD // VH
    local_heads = local_width // head_dim
    grouped = vis_qkv.reshape(frames_dev, 4 * FT, 3, local_heads, head_dim)
    vit_scores = jnp.einsum(
        "fqhd,fkhd->fhqk", grouped[:, :, 0], grouped[:, :, 1], preferred_element_type=jnp.float32
    ) / math.sqrt(head_dim)
    vit_max = jnp.max(vit_scores, axis=3, keepdims=True)
    vit_exp = jnp.exp(vit_scores - vit_max)
    vit_total = jnp.sum(vit_exp, axis=3, keepdims=True)
    vit_mixed = jnp.einsum(
        "fhqk,fkhd->fqhd",
        vit_exp.astype(jnp.bfloat16),
        grouped[:, :, 2],
        preferred_element_type=jnp.float32,
    )
    context = (
        (vit_mixed / jnp.transpose(vit_total, (0, 2, 1, 3)))
        .astype(jnp.bfloat16)
        .reshape(patches, local_width)
    )
    hidden = vis_resid.astype(jnp.float32) + jnp.dot(
        lax.all_gather(context, "tp", axis=1, tiled=True),
        vis_out_w,
        preferred_element_type=jnp.float32,
    )
    row_sum, row_squares = lax.psum(
        (jnp.sum(hidden, axis=1), jnp.sum(hidden * hidden, axis=1)), "tp"
    )
    mean_value = row_sum / VD
    variance = row_squares / VD - mean_value * mean_value
    normed = (
        (hidden - mean_value[:, None]) * lax.rsqrt(variance + 1e-06)[:, None] * merge_gain
        + merge_bias
    ).astype(jnp.bfloat16)
    merged = normed.reshape(frames_dev * FT, 4, local_width)
    sending, placing, filled = frame_tables(frame_host, vis_pos, device, per_device, frames_dev)
    local_kv = vis_kv_w.shape[2] // lax.axis_size("tp")
    own_features = merged.reshape(frames_dev, FT * 4 * local_width)
    outgoing = jnp.dot(sending, own_features, preferred_element_type=jnp.float32).astype(
        jnp.bfloat16
    )
    received = passed_along(outgoing, "ctx", peers // 2)
    sources = jnp.concatenate([own_features, received], axis=0)
    arrived_features = jnp.dot(placing, sources, preferred_element_type=jnp.float32)
    arrived_features = arrived_features.astype(jnp.bfloat16).reshape(per_device, 4, local_width)
    arrived = jnp.transpose(
        lax.psum_scatter(
            jnp.einsum(
                "jcr,tjc->rt", vis_kv_w, arrived_features, preferred_element_type=jnp.float32
            ),
            "tp",
            scatter_dimension=0,
            tiled=True,
        )
    ).astype(jnp.bfloat16)
    filled_rows = jnp.repeat(filled, FT)
    kv_heads = local_kv // (2 * HD)
    keys_values = jnp.where(
        filled_rows[:, None], arrived, text_kv.reshape(per_device, local_kv)
    ).reshape(per_device, kv_heads, 2, HD)
    group = H // KVH
    query_rows = queries.reshape(per_device, kv_heads, group, HD)
    first_pos = device * per_device
    last_pos = first_pos + per_device - 1
    query_pos = first_pos + jnp.arange(per_device, dtype=jnp.int32)
    query_doc = lax.dynamic_slice_in_dim(doc_ids, first_pos, per_device)
    score_scale = 1.0 / math.sqrt(HD)
    initial = (
        jnp.full((per_device, kv_heads, group), NEGATIVE, jnp.float32),
        jnp.zeros((per_device, kv_heads, group), jnp.float32),
        jnp.zeros((per_device, kv_heads, group, HD), jnp.float32),
    )
    carry = initial
    key_piece = lax.all_gather(keys_values, "ctx", axis=0, tiled=True)
    row_count = key_piece.shape[0]
    block_rows = math.gcd(row_count, 512)
    block_count = row_count // block_rows
    key_blocks = key_piece.reshape(block_count, block_rows, kv_heads, 2, HD)

    def one_block(softmax_state, packed):
        key_block, block_index = packed
        key_start = block_index * block_rows

        def update(state_in):
            row_max, exp_total, accum = state_in
            key_pos = key_start + jnp.arange(block_rows, dtype=jnp.int32)
            key_doc = lax.dynamic_slice_in_dim(doc_ids, jnp.maximum(key_start, 0), block_rows)
            allowed = (key_pos[None, :] <= query_pos[:, None]) & (
                key_doc[None, :] == query_doc[:, None]
            )
            allowed_full = allowed[:, None, None, :]
            scores = (
                jnp.einsum(
                    "tkgd,skd->tkgs",
                    query_rows,
                    key_block[:, :, 0],
                    preferred_element_type=jnp.float32,
                )
                * score_scale
            )
            new_max = jnp.maximum(
                row_max, jnp.max(jnp.where(allowed_full, scores, NEGATIVE), axis=3)
            )
            exponent = jnp.where(allowed_full, jnp.exp(scores - new_max[..., None]), 0.0)
            factor = jnp.exp(row_max - new_max)
            new_total = exp_total * factor + jnp.sum(exponent, axis=3)
            new_accum = accum * factor[..., None] + jnp.einsum(
                "tkgs,skd->tkgd",
                exponent.astype(jnp.bfloat16),
                key_block[:, :, 1],
                preferred_element_type=jnp.float32,
            )
            return (new_max, new_total, new_accum)

        skipped = (key_start > last_pos) | (key_start < 0)
        return (lax.cond(skipped, lambda unchanged: unchanged, update, softmax_state), None)

    carry, _ = lax.scan(one_block, carry, (key_blocks, jnp.arange(block_count, dtype=jnp.int32)))
    row_max, exp_total, accum = carry
    return (
        (accum / exp_total[..., None])
        .astype(jnp.bfloat16)
        .reshape(per_device, kv_heads * group * HD)
    )


def solution(mesh):
    return jax.shard_map(
        shards,
        mesh=mesh,
        in_specs=(
            P(("dp", "ctx"), None, "tp"),
            P(("dp", "ctx"), "tp"),
            P(None, "tp"),
            P("tp"),
            P("tp"),
            P(None, "tp", None),
            P("dp"),
            P("dp"),
            P("dp"),
            P(("dp", "ctx"), "tp", None, None),
            P(("dp", "ctx"), "tp"),
        ),
        out_specs=P(("dp", "ctx"), "tp"),
        check_vma=False,
    )
```

profile of v0, /device:TPU:248, one launch (start us, length us, event | category | flops | bytes accessed | tf_op | source)
XLA Modules:
  0.0 637.6 jit_solution(9065145647898950215)
XLA Ops:
  6.5 1.6 multiply_reduce_fusion
  8.6 2.1 fusion.22
  12.5 88.6 %all-gather.3.cloned.1.call-done = bf16[512,1280]{0,1:T(8,128)(2,1)} async-done(((bf16[512,160]{0,1:T(8,128)(2,1)}), bf16[512,1280]{0,1:T(8,128)(2,1)}) %all-gather.3.cloned.1.call-update) | async-done | bytes 1310736 | tf_op jit(solution)/shard_map/all_gather | solution.py:98
  101.1 1.7 fusion.36
  102.9 40.7 %all-reduce = (f32[512]{0:T(512)S(1)}, f32[512]{0:T(512)S(1)}) all-reduce(f32[512]{0:T(512)S(1)} %get-tuple-element.181, f32[512]{0:T(512)S(1)} %get-tuple-element.180), channel_id=1, replica_groups=mesh['ctx'=32,'tp'=8,'dp'=2] {'tp'}, use_global_device_ids=true, to_apply=%region_9.10 | all-reduce | flops 1024 | bytes 8192 | tf_op jit(solution)/shard_map/psum | solution.py:102
  144.3 3.7 collective-permute-start
  148.4 1.2 reshape_reshape.3
  149.5 25.9 %collective-permute-done = bf16[1,81920]{1,0:T(2,128)(2,1)} collective-permute-done((bf16[1,81920]{1,0:T(2,128)(2,1)S(1)}, bf16[1,81920]{1,0:T(2,128)(2,1)}, u32[]{:S(2)}, u32[]{:S(2)}) %collective-permute-start) | collective-permute-done | bytes 163872 | tf_op jit(solution)/shard_map/ppermute | solution.py:22
  175.4 1.9 convolution_convert_fusion
  177.9 2.4 convolution_bitcast_fusion.1
  180.4 137.6 %reduce-scatter.2.cloned.1.call-done = f32[256,256]{0,1:T(8,128)} async-done(((f32[2048,256]{0,1:T(8,128)}), f32[256,256]{0,1:T(8,128)}) %reduce-scatter.2.cloned.1.call-update) | async-done | bytes 262160 | tf_op jit(solution)/shard_map/reduce_scatter | solution.py:123
  318.0 1.0 bitcast_select_fusion.1
  320.9 225.5 %all-gather.5.cloned.1.call-done = bf16[8192,1,2,128]{3,0,2,1:T(8,128)(2,1)} async-done(((bf16[256,1,2,128]{3,0,2,1:T(8,128)(2,1)}), bf16[8192,1,2,128]{3,0,2,1:T(8,128)(2,1)}) %all-gather.5.cloned.1.call-update) | async-done | bytes 4194320 | tf_op jit(solution)/shard_map/all_gather | solution.py:150
  546.4 4.6 copy.36
  551.0 79.2 %while.15 = (s32[]{:T(128)}, f32[256,1,4]{0,2,1:T(4,128)S(1)}, f32[256,1,4]{0,2,1:T(4,128)S(1)}, f32[256,1,4,128]{0,3,2,1:T(8,128)S(1)}, s32[16]{0:T(128)S(1)}, ...) while((s32[]{:T(128)}, f32[256,1,4]{0,2,1:T(4,128)S(1)}, ...), condition=%wide.region_17.18_spmd.clone, body=%wide.region_12.17_spmd.clone.sunk | while | flops 274861824 | bytes 8994139 | solution.py:194
  552.3 3.7 conditional.3
  552.3 0.8 dynamic_slice.14
  553.3 1.0 dynamic-slice_bitcast_fusion
  557.2 3.7 conditional.3
  557.3 0.8 dynamic_slice.14
  558.3 1.0 dynamic-slice_bitcast_fusion
  562.2 3.7 conditional.3
  562.2 0.8 dynamic_slice.14
  563.2 1.0 dynamic-slice_bitcast_fusion
  567.1 3.6 conditional.3
  567.2 0.8 dynamic_slice.14
  568.2 1.0 dynamic-slice_bitcast_fusion
  572.1 3.7 conditional.3
  572.1 0.8 dynamic_slice.14
  573.1 1.0 dynamic-slice_bitcast_fusion
  577.0 3.7 conditional.3
  577.1 0.8 dynamic_slice.14
  578.1 1.0 dynamic-slice_bitcast_fusion
  582.0 3.7 conditional.3
  582.0 0.8 dynamic_slice.14
  583.0 1.0 dynamic-slice_bitcast_fusion
  586.9 3.7 conditional.3
  587.0 0.8 dynamic_slice.14
  588.0 1.0 dynamic-slice_bitcast_fusion
  591.9 3.6 conditional.3
  591.9 0.8 dynamic_slice.14
  592.9 1.0 dynamic-slice_bitcast_fusion
  596.8 3.7 conditional.3
  596.9 0.8 dynamic_slice.14
  597.9 1.0 dynamic-slice_bitcast_fusion
  601.8 3.7 conditional.3
  601.8 0.8 dynamic_slice.14
  602.8 1.0 dynamic-slice_bitcast_fusion
  606.7 3.7 conditional.3
  606.8 0.8 dynamic_slice.14
  607.8 1.0 dynamic-slice_bitcast_fusion
  611.7 3.7 conditional.3
  611.7 0.8 dynamic_slice.14
  612.7 1.0 dynamic-slice_bitcast_fusion
  616.6 3.6 conditional.3
  616.7 0.8 dynamic_slice.14
  617.7 1.0 dynamic-slice_bitcast_fusion
  621.6 3.6 conditional.3
  621.6 0.8 dynamic_slice.14
  622.6 1.0 dynamic-slice_bitcast_fusion
  626.5 3.6 conditional.3
  626.5 0.8 dynamic_slice.14
  627.5 1.0 dynamic-slice_bitcast_fusion
  630.3 0.8 copy.43
  (227 shorter events, 44.1 us)
Async XLA Ops:
  6.5 171.4 %copy-start = (bf16[4,160,2048]{2,1,0:T(8,128)(2,1)S(1)}, bf16[4,160,2048]{2,1,0:T(8,128)(2,1)}, u32[]{:S(2)}) copy-start(bf16[4,160,2048]{2,1,0:T(8,128)(2,1)} %param.20) | copy-start | bytes 7864324
  6.5 94.6 %all-gather.3.cloned.1.call-start = ((), (), s32[]{:S(2)}) async-start(), calls=%async_computation.1 | async-start | bytes 1474560 | tf_op jit(solution)/shard_map/all_gather | solution.py:98
  8.5 2.3 copy-start.8
  8.6 2.3 copy-start.5
  8.6 92.6 %copy-start.1 = (bf16[1280,160]{0,1:T(8,128)(2,1)S(1)}, bf16[1280,160]{0,1:T(8,128)(2,1)}, u32[]{:S(2)}) copy-start(bf16[1280,160]{0,1:T(8,128)(2,1)} %param.17) | copy-start | bytes 1228804
  8.6 92.6 %copy-start.3 = (bf16[512,160]{0,1:T(8,128)(2,1)S(1)}, bf16[512,160]{0,1:T(8,128)(2,1)}, u32[]{:S(2)}) copy-start(bf16[512,160]{0,1:T(8,128)(2,1)} %param.16) | copy-start | bytes 491524
  8.6 135.0 %copy-start.6 = (f32[160]{0:T(256)S(1)}, f32[160]{0:T(256)}, u32[]{:S(2)}) copy-start(f32[160]{0:T(256)} %param.19) | copy-start | bytes 1924
  8.6 135.0 %copy-start.7 = (f32[160]{0:T(256)S(1)}, f32[160]{0:T(256)}, u32[]{:S(2)}) copy-start(f32[160]{0:T(256)} %param.18) | copy-start | bytes 1924
  10.8 307.2 %reduce-scatter.2.cloned.1.call-start = ((), (), s32[]{:S(2)}) async-start(), calls=%async_computation.2 | async-start | bytes 2359296 | tf_op jit(solution)/shard_map/reduce_scatter | solution.py:123
  144.3 31.1 %collective-permute-start = (bf16[1,81920]{1,0:T(2,128)(2,1)S(1)}, bf16[1,81920]{1,0:T(2,128)(2,1)}, u32[]{:S(2)}, u32[]{:S(2)}) collective-permute-start(bf16[1,81920]{1,0:T(2,128)(2,1)S(1)} %convert_element_type.53), channel_id=1, source_target_pairs={{256,0},{272,16},{288,32},{304,48},{320,64},{336,80},{352,96},{368... | collective-permute-start | bytes 491528 | tf_op jit(solution)/shard_map/ppermute | solution.py:22
  180.3 137.7 %copy-start.4 = (bf16[256,1,2,128]{3,2,1,0:T(2,128)(2,1)S(1)}, bf16[256,1,2,128]{3,2,1,0:T(2,128)(2,1)}, u32[]{:S(2)}) copy-start(bf16[256,1,2,128]{3,2,1,0:T(2,128)(2,1)} %param.24) | copy-start | bytes 393220
  180.3 139.5 %copy-start.2 = (bf16[256,512]{1,0:T(8,128)(2,1)S(1)}, bf16[256,512]{1,0:T(8,128)(2,1)}, u32[]{:S(2)}) copy-start(bf16[256,512]{1,0:T(8,128)(2,1)} %param.25) | copy-start | bytes 786436
  180.3 366.1 %all-gather.5.cloned.1.call-start = ((), (), s32[]{:S(2)}) async-start(), calls=%async_computation.3 | async-start | bytes 4325376 | tf_op jit(solution)/shard_map/all_gather | solution.py:150
Sparse Core Ops, SparseCore 0:
  10.9 90.1 all-gather.2
  180.4 137.5 reduce-scatter.1
  320.3 226.0 all-gather.4
where the time goes:
time: 639 us; the launch traced here: 638 us
  waiting for transfers between devices  478 us (75%)
  local copies, waits for them, and re-layouts  47.2 us (7%)
  blocking collectives  40.7 us (6%)
  matrix products  28.2 us (4%)
  other arithmetic  14 us (2%)
  between operations  14 us (2%)
  loops' own time  12.1 us (2%)
    all_gather x1, waiting for transfers between devices, shards(): key_piece = lax.all_gather(keys_values, 'ctx', axis=0, tiled=True)  225 us
    reduce_scatter x1, waiting for transfers between devices, shards(): lax.psum_scatter(jnp.einsum('jcr,tjc->rt', vis_kv_w, arrived_features, pr...  138 us
    all_gather x1, waiting for transfers between devices, shards(): lax.all_gather(context, 'tp', axis=1, tiled=True)  88.6 us
    psum x1, blocking collectives, shards(): lax.psum((jnp.sum(hidden, axis=1), jnp.sum(hidden * hidden, axis=1)), 'tp')  40.7 us
    ppermute x1, waiting for transfers between devices, passed_along(): return lax.ppermute(block, axis, route)  25.9 us
    squeeze x16, local copies, waits for them, and re-layouts, shards(): lax.scan(one_block, carry, (key_blocks, jnp.arange(block_count, dtype=jnp...  15.6 us
  transfers between devices with their start and end apart: 4, of which 4 were waited for; matrix products, arithmetic and copies ran while one was open for 1% of the time, Pallas kernels for 0%

commit v1 on v0

v1 whole, which is shorter than its diff:
```python
import functools
import math

import jax
import jax.numpy as jnp
from jax import lax
from jax.experimental import pallas as pl
from jax.experimental.pallas import tpu as pltpu
from jax.sharding import PartitionSpec as P

VD = 1280
VH = 16
HD = 128
FT = 128
FP = 512
T = 256
GROUP = 4
LOCAL = 160
HEAD = 80
CTX = 32
TP = 8
NEGATIVE = -1e30
LOG2E = math.log2(math.e)
MESH = pl.DeviceIdType.MESH
F32 = jnp.float32
BF16 = jnp.bfloat16


def dot_nt(a, b):
    return lax.dot_general(a, b, (((1,), (1,)), ((), ())), preferred_element_type=F32)


def dot_nn(a, b):
    return lax.dot_general(a, b, (((1,), (0,)), ((), ())), preferred_element_type=F32)


def eye(rows, cols, dtype):
    r = lax.broadcasted_iota(jnp.int32, (rows, cols), 0)
    c = lax.broadcasted_iota(jnp.int32, (rows, cols), 1)
    return jnp.where(r == c, 1.0, 0.0).astype(dtype)


class Gather:
    def __init__(self, buf, send_z, send_f, send_y, recv, place):
        self.buf, self.send_z, self.send_f, self.send_y, self.recv = buf, send_z, send_f, send_y, recv
        self.zl, self.y, self.tp, self.dp = place
        self.me = self.zl * 4 + self.y
        self.quad = (self.zl // 4) * 4
        self.far = lax.rem(self.zl + 4, 8)
        self.far_quad = 4 - self.quad
        self.sent = []

    def copy(self, block, sem, zl, y):
        return pltpu.make_async_remote_copy(
            src_ref=self.buf.at[block],
            dst_ref=self.buf.at[block],
            send_sem=sem,
            recv_sem=self.recv.at[block],
            device_id=(zl * 4 + y, self.tp, self.dp),
            device_id_type=MESH,
        )

    def wait_block(self, block):
        self.copy(block, self.send_z.at[0], self.far, self.y).wait_recv()

    def near(self, d):
        return self.quad + lax.rem(self.zl + d, 4)

    def start(self, copy):
        copy.start()
        self.sent.append(copy)

    def spread_y(self, slot, block):
        for d in (1, 3, 2):
            self.start(self.copy(block, self.send_y.at[slot * 3 + d - 1], self.zl, lax.rem(self.y + d, 4)))

    def first(self):
        self.start(self.copy(self.me, self.send_z.at[0], self.far, self.y))
        for d in (1, 2, 3):
            self.start(self.copy(self.me, self.send_z.at[d], self.near(d), self.y))
        self.spread_y(0, self.me)

    def take_near(self):
        for d in (1, 2, 3):
            block = self.near(d) * 4 + self.y
            self.wait_block(block)
            self.spread_y(d, block)

    def take_far(self):
        block = self.far * 4 + self.y
        self.wait_block(block)
        for d in (1, 2, 3):
            self.start(self.copy(block, self.send_f.at[d - 1], self.near(d), self.y))
        self.spread_y(4, block)

    def take_rest(self):
        for d in (1, 2, 3):
            block = (self.far_quad + lax.rem(self.zl + d, 4)) * 4 + self.y
            self.wait_block(block)
            self.spread_y(4 + d, block)

    def take_y(self):
        def layer(z, carry):
            for d in (1, 2, 3):
                self.wait_block(z * 4 + lax.rem(self.y + d, 4))
            return carry

        lax.fori_loop(0, 8, layer, 0)

    def finish(self):
        for copy in self.sent:
            copy.wait_send()


def kernel(
    qkv, resid, out_w, gain, bias, kv_w_hbm, host, pos, docs, text, queries,
    out,
    kv_w, ctx, mine, stat, part_send, part_recv, part_own, pair_send, pair_recv, perm,
    tbuf, vbuf, text_pos, frame_pos, m_s, l_s, acc_s,
    load_sem, cz_s, cz_r, cx_s, cx_r, cf_s, cf_r, st_s, st_r, rx_s, rx_r, rz_s, rz_r,
    tz_s, tf_s, ty_s, t_r, vz_s, vf_s, vy_s, v_r,
):
    c = lax.axis_index("ctx")
    tp = lax.axis_index("tp")
    dp = lax.axis_index("dp")
    zl, y = c // 4, lax.rem(c, 4)
    zh, x = tp // 4, lax.rem(tp, 4)
    other = 1 - zh

    def at_tp(h, col):
        return (c, h * 4 + col, dp)

    def x_of(d):
        return lax.rem(x + d, 4)

    barrier = pltpu.get_barrier_semaphore()
    for d in range(1, TP):
        pl.semaphore_signal(barrier, inc=1, device_id=(c, lax.rem(tp + d, TP), dp), device_id_type=MESH)
    for d in range(1, 8):
        pl.semaphore_signal(barrier, inc=1, device_id=(lax.rem(zl + d, 8) * 4 + y, tp, dp), device_id_type=MESH)
    for d in range(1, 4):
        pl.semaphore_signal(barrier, inc=1, device_id=(zl * 4 + lax.rem(y + d, 4), tp, dp), device_id_type=MESH)

    load = pltpu.make_async_copy(kv_w_hbm, kv_w, load_sem.at[0])
    load.start()
    load_text = pltpu.make_async_copy(text, tbuf.at[c], load_sem.at[1])
    load_text.start()

    texts = Gather(tbuf, tz_s, tf_s, ty_s, t_r, (zl, y, tp, dp))
    frames = Gather(vbuf, vz_s, vf_s, vy_s, v_r, (zl, y, tp, dp))

    keys = dot_nt(eye(FP, FP, BF16), qkv[1]).astype(BF16)
    sent = []
    rows_of = lambda t, h: pl.ds(pl.multiple_of(t * LOCAL + h * HEAD, 16), HEAD)

    def ctx_copy(t, h, send, recv, target):
        return pltpu.make_async_remote_copy(
            src_ref=ctx.at[rows_of(t, h)],
            dst_ref=ctx.at[rows_of(t, h)],
            send_sem=send,
            recv_sem=recv,
            device_id=target,
            device_id_type=MESH,
        )

    def begin(copy):
        copy.start()
        sent.append(copy)

    for h in range(2):
        head = slice(h * HEAD, (h + 1) * HEAD)
        scores = dot_nn(keys[:, head], qkv[0, head, :]) * (LOG2E / math.sqrt(HEAD))
        top = jnp.max(scores, axis=0, keepdims=True)
        weights = jnp.exp2(scores - top)
        total = jnp.sum(weights, axis=0, keepdims=True)
        mixed = dot_nn(qkv[2, head, :], weights.astype(BF16)) / total
        ctx[rows_of(tp, h), :] = mixed.astype(BF16)
        if h == 0:
            pl.semaphore_wait(barrier, TP - 1 + 7 + 3)
        begin(ctx_copy(tp, h, cz_s.at[h], cz_r.at[h], at_tp(other, x)))
        for d in (1, 3, 2):
            begin(ctx_copy(tp, h, cx_s.at[h * 3 + d - 1], cx_r.at[h * 3 + d - 1], at_tp(zh, x_of(d))))

    load_text.wait()
    texts.first()

    slot = lax.broadcasted_iota(jnp.int32, (64, 32), 0) * FT
    held = jnp.max(jnp.where(slot == pos[...], 1, 0), axis=1, keepdims=True)
    slot_col = lax.broadcasted_iota(jnp.int32, (64, 1), 0) * FT
    text_pos[...] = jnp.broadcast_to(jnp.where(held > 0, -1 << 20, slot_col), (64, 128))
    owner = lax.broadcasted_iota(jnp.int32, (CTX, 32), 0)
    frame_col = jnp.sum(jnp.where(owner == host[...], pos[...], 0), axis=1, keepdims=True)
    frame_pos[...] = jnp.broadcast_to(frame_col, (CTX, 128))
    doc = jnp.concatenate([docs[pl.ds(2 * c, 1), :], docs[pl.ds(2 * c + 1, 1), :]], axis=1)
    first = jnp.zeros((1, T), jnp.int32)
    for d in (1, 2, 3):
        before = jnp.sum(jnp.where(docs[...] < d, 1, 0), axis=(0, 1), keepdims=True)
        first = jnp.where(doc == d, before, first)
    query_pos = c * T + lax.broadcasted_iota(jnp.int32, (1, T), 1)
    m_s[...] = jnp.full(m_s.shape, NEGATIVE, F32)
    l_s[...] = jnp.zeros(l_s.shape, F32)
    acc_s[...] = jnp.zeros(acc_s.shape, F32)

    def attend(kv, key_pos, causal):
        k = kv[:, :HD]
        vt = kv[:, HD:].T
        allowed = key_pos >= first
        if causal:
            allowed = allowed & (key_pos <= query_pos)
        for g in range(GROUP):
            scores = dot_nt(k, queries[:, g * HD : (g + 1) * HD]) * (LOG2E / math.sqrt(HD))
            scores = jnp.where(allowed, scores, NEGATIVE)
            old = m_s[g : g + 1, :]
            new = jnp.maximum(old, jnp.max(scores, axis=0, keepdims=True))
            weights = jnp.exp2(scores - new)
            factor = jnp.exp2(old - new)
            m_s[g : g + 1, :] = new
            l_s[g : g + 1, :] = l_s[g : g + 1, :] * factor + jnp.sum(weights, axis=0, keepdims=True)
            acc_s[g] = acc_s[g] * factor + dot_nn(vt, weights.astype(BF16))

    within = lax.broadcasted_iota(jnp.int32, (FT, T), 0)

    def two(a, b):
        return jnp.concatenate([within + jnp.concatenate([a, a], axis=1), within + jnp.concatenate([b, b], axis=1)], axis=0)

    def text_block(b, causal):
        attend(tbuf[b], two(text_pos[pl.ds(2 * b, 1), :], text_pos[pl.ds(2 * b + 1, 1), :]), causal)

    def text_range(lo, hi):
        def step(b, carry):
            text_block(b, False)
            return carry

        lax.fori_loop(lo, hi, step, 0)

    r = lax.broadcasted_iota(jnp.int32, (FP, FP), 0)
    p = lax.broadcasted_iota(jnp.int32, (FP, FP), 1)
    perm[...] = jnp.where((r % FT) * 4 + r // FT == p, 1.0, 0.0).astype(BF16)
    gain_col = jnp.sum(jnp.where(eye(LOCAL, LOCAL, F32) > 0, gain[...], 0.0), axis=1, keepdims=True)
    bias_col = jnp.sum(jnp.where(eye(LOCAL, LOCAL, F32) > 0, bias[...], 0.0), axis=1, keepdims=True)

    texts.take_near()
    for h in range(2):
        ctx_copy(other * 4 + x, h, cz_s.at[h], cz_r.at[h], at_tp(other, x)).wait_recv()
        for d in (1, 3, 2):
            begin(ctx_copy(other * 4 + x, h, cf_s.at[h * 3 + d - 1], cf_r.at[h * 3 + d - 1], at_tp(zh, x_of(d))))
    texts.take_far()
    for h in range(2):
        for d in (1, 2, 3):
            ctx_copy(zh * 4 + x_of(4 - d), h, cx_s.at[0], cx_r.at[h * 3 + d - 1], at_tp(zh, x_of(d))).wait_recv()
    half = lambda i: pl.ds(pl.multiple_of(i * (VD // 2), 128), VD // 2)
    hidden = resid[...].astype(F32) + dot_nn(out_w[:, half(zh)], ctx[half(zh), :])
    for h in range(2):
        for d in (1, 2, 3):
            ctx_copy(other * 4 + x_of(4 - d), h, cf_s.at[0], cf_r.at[h * 3 + d - 1], at_tp(zh, x_of(d))).wait_recv()
    hidden = hidden + dot_nn(out_w[:, half(other)], ctx[half(other), :])
    mine[...] = hidden

    sums = jnp.sum(hidden, axis=0, keepdims=True)
    squares = jnp.sum(hidden * hidden, axis=0, keepdims=True)
    for i in range(4):
        stat[tp, i : i + 1, :] = sums[:, i * 128 : (i + 1) * 128]
        stat[tp, 4 + i : 5 + i, :] = squares[:, i * 128 : (i + 1) * 128]

    def stat_copy(t, d, target):
        return pltpu.make_async_remote_copy(
            src_ref=stat.at[t],
            dst_ref=stat.at[t],
            send_sem=st_s.at[d - 1],
            recv_sem=st_r.at[d - 1],
            device_id=(c, target, dp),
            device_id_type=MESH,
        )

    for d in range(1, TP):
        begin(stat_copy(tp, d, lax.rem(tp + d, TP)))
    texts.take_rest()
    for d in range(1, TP):
        stat_copy(lax.rem(tp + TP - d, TP), d, lax.rem(tp + d, TP)).wait_recv()
    all_stats = stat[0]
    for t in range(1, TP):
        all_stats = all_stats + stat[t]
    mean = all_stats[0:4] * (1.0 / VD)
    scale = lax.rsqrt(all_stats[4:8] * (1.0 / VD) - mean * mean + 1e-6)
    mean_row = jnp.concatenate([mean[i : i + 1] for i in range(4)], axis=1)
    scale_row = jnp.concatenate([scale[i : i + 1] for i in range(4)], axis=1)
    normed = ((mine[...] - mean_row) * scale_row * gain_col + bias_col).astype(BF16)
    grouped = dot_nt(perm[...], normed).astype(BF16)

    load.wait()

    def partial_kv(t):
        cols = pl.ds(pl.multiple_of(t * 2 * HD, 128), 2 * HD)
        total = dot_nn(grouped[:FT], kv_w[0, :, cols])
        for j in range(1, 4):
            total = total + dot_nn(grouped[j * FT : (j + 1) * FT], kv_w[j, :, cols])
        return total

    def part_copy(d):
        return pltpu.make_async_remote_copy(
            src_ref=part_send.at[d - 1],
            dst_ref=part_recv.at[d - 1],
            send_sem=rx_s.at[d - 1],
            recv_sem=rx_r.at[d - 1],
            device_id=at_tp(zh, x_of(d)),
            device_id_type=MESH,
        )

    for d in (2, 1, 3):
        for i in range(2):
            part_send[d - 1, i] = partial_kv(i * 4 + x_of(d)).astype(BF16)
        begin(part_copy(d))
    part_own[0] = partial_kv(other * 4 + x)
    part_own[1] = partial_kv(zh * 4 + x)
    for d in (1, 2, 3):
        part_copy(d).wait_recv()

    def summed(slot, which):
        total = part_own[slot]
        for d in range(3):
            total = total + part_recv[d, which].astype(F32)
        return total

    pair_send[...] = summed(0, other).astype(BF16)
    pair = pltpu.make_async_remote_copy(
        src_ref=pair_send,
        dst_ref=pair_recv,
        send_sem=rz_s.at[0],
        recv_sem=rz_r.at[0],
        device_id=at_tp(other, x),
        device_id_type=MESH,
    )
    begin(pair)
    part_own[1] = summed(1, zh)

    texts.take_y()
    middle = c // 2
    text_range(0, middle)
    pair.wait_recv()
    vbuf[c] = (part_own[1] + pair_recv[...].astype(F32)).astype(BF16)
    frames.first()
    text_range(middle, c)
    text_block(c, True)
    frames.take_near()
    frames.take_far()
    frames.take_rest()
    frames.take_y()

    def frame_step(i, carry):
        kv = jnp.concatenate([vbuf[i], vbuf[i + 16]], axis=0)
        attend(kv, two(frame_pos[pl.ds(i, 1), :], frame_pos[pl.ds(i + 16, 1), :]), True)
        return carry

    lax.fori_loop(0, jnp.minimum(c, 15) + 1, frame_step, 0)

    for g in range(GROUP):
        result = (acc_s[g] / l_s[g : g + 1, :]).astype(BF16)
        out[:, g * HD : (g + 1) * HD] = dot_nt(eye(T, T, BF16), result).astype(BF16)
    for copy in sent:
        copy.wait_send()
    texts.finish()
    frames.finish()


def shards(
    vis_qkv, vis_resid, vis_out_w, merge_gain, merge_bias, vis_kv_w, frame_host, vis_pos, doc_ids, text_kv, queries
):
    vmem = pl.BlockSpec(memory_space=pltpu.VMEM)
    hbm = pl.BlockSpec(memory_space=pl.ANY)
    dma = lambda n: pltpu.SemaphoreType.DMA((n,))
    return pl.pallas_call(
        kernel,
        out_shape=jax.ShapeDtypeStruct((T, GROUP * HD), BF16),
        in_specs=[vmem, vmem, vmem, vmem, vmem, hbm, vmem, vmem, vmem, hbm, vmem],
        out_specs=vmem,
        scratch_shapes=[
            pltpu.VMEM((4, LOCAL, 8 * 2 * HD), BF16),
            pltpu.VMEM((VD, FP), BF16),
            pltpu.VMEM((LOCAL, FP), F32),
            pltpu.VMEM((TP, 8, 128), F32),
            pltpu.VMEM((3, 2, FT, 2 * HD), BF16),
            pltpu.VMEM((3, 2, FT, 2 * HD), BF16),
            pltpu.VMEM((2, FT, 2 * HD), F32),
            pltpu.VMEM((FT, 2 * HD), BF16),
            pltpu.VMEM((FT, 2 * HD), BF16),
            pltpu.VMEM((FP, FP), BF16),
            pltpu.VMEM((CTX, T, 2 * HD), BF16),
            pltpu.VMEM((CTX, FT, 2 * HD), BF16),
            pltpu.VMEM((64, 128), jnp.int32),
            pltpu.VMEM((CTX, 128), jnp.int32),
            pltpu.VMEM((8, T), F32),
            pltpu.VMEM((8, T), F32),
            pltpu.VMEM((GROUP, HD, T), F32),
            dma(2), dma(2), dma(2), dma(6), dma(6), dma(6), dma(6), dma(7), dma(7), dma(3), dma(3), dma(1), dma(1),
            dma(4), dma(3), dma(24), dma(CTX), dma(4), dma(3), dma(24), dma(CTX),
        ],
        compiler_params=pltpu.CompilerParams(collective_id=0, has_side_effects=True, vmem_limit_bytes=48 * 2**20),
        name="window",
    )(
        jnp.transpose(vis_qkv, (1, 2, 0)),
        jnp.transpose(vis_resid),
        jnp.transpose(vis_out_w),
        merge_gain.reshape(1, LOCAL),
        merge_bias.reshape(1, LOCAL),
        vis_kv_w,
        frame_host.reshape(1, 32),
        vis_pos.reshape(1, 32),
        doc_ids.reshape(64, 128),
        text_kv.reshape(T, 2 * HD),
        queries,
    )


def solution(mesh):
    return jax.shard_map(
        shards,
        mesh=mesh,
        in_specs=(
            P(("dp", "ctx"), None, "tp"),
            P(("dp", "ctx"), "tp"),
            P(None, "tp"),
            P("tp"),
            P("tp"),
            P(None, "tp", None),
            P("dp"),
            P("dp"),
            P("dp"),
            P(("dp", "ctx"), "tp", None, None),
            P(("dp", "ctx"), "tp"),
        ),
        out_specs=P(("dp", "ctx"), "tp"),
        check_vma=False,
    )
```

time: 639 us -> 178 us (0.28)
  the two profiles are of different devices: /device:TPU:248 before, /device:TPU:232 now
where the time goes in v1:
time: 178 us
  Pallas kernels  167 us (94%)
  local copies, waits for them, and re-layouts  10.7 us (6%)
    pallas_call x1, Pallas kernels, shards(): pl.pallas_call(kernel, out_shape=jax.ShapeDtypeStruct((T, GROUP * HD), BF...  167 us
    unnamed x22, local copies, waits for them, and re-layouts  10.7 us

profile of v1, /device:TPU:232, one launch (start us, length us, event | category | flops | bytes accessed | tf_op | source)
XLA Modules:
  0.0 177.8 jit_solution(7361730018990479774)
XLA Ops:
  0.0 0.9 copy.14
  0.9 0.0 copy-start
  0.9 1.7 copy-done
  2.7 0.0 copy-start.1
  2.7 1.0 copy-done.1
  3.7 0.0 copy-start.2
  3.7 1.0 copy-done.2
  4.7 0.0 copy-start.3
  4.7 0.9 copy-done.3
  5.7 0.0 copy-start.4
  5.7 0.9 copy-done.4
  6.6 0.0 copy-start.5
  6.6 0.8 copy-done.5
  7.3 0.0 copy-start.6
  7.3 0.7 copy-done.6
  8.0 0.0 copy-start.7
  8.0 0.7 copy-done.7
  8.7 0.0 copy-start.8
  8.7 0.7 copy-done.8
  9.3 0.0 copy-start.9
  9.3 0.7 copy-done.9
  10.0 167.1 %window.1 = bf16[256,512]{1,0:T(8,128)(2,1)S(1)} custom-call(bf16[3,160,512]{2,1,0:T(8,128)(2,1)S(1)} %bitcast.14, bf16[160,512]{1,0:T(8,128)(2,1)S(1)} %bitcast.16, bf16[160,1280]{1,0:T(8,128)(2,1)S(1)} %bitcast.15, f32[1,160]{1,0:T(1,128)S(1)} %bitcast.18, f32[1,160]{1,0:T(1,128)S(1)} %bitcast.19, bf16[4,160,2048]{2,1,0:T(8,128)(2,1)S(1)} %copy-done, ...), custom_call_target="tpu_custom_call" | custom-call | tf_op jit(solution)/shard_map/window/pallas_call | solution.py:371
  177.1 0.7 copy.16
Async XLA Ops:
  0.9 1.7 copy-start
  2.7 1.0 copy-start.1
  3.7 1.0 copy-start.2
  4.7 0.9 copy-start.3
  5.7 0.9 copy-start.4
  6.6 0.8 copy-start.5
  7.3 0.7 copy-start.6
  8.0 0.7 copy-start.7
  8.7 0.7 copy-start.8
  9.3 0.7 copy-start.9

commit v2 on v1

--- a/solution.py
+++ b/solution.py
@@ -40,14 +40,10 @@
     return jnp.where(r == c, 1.0, 0.0).astype(dtype)
 
 
-class Gather:
-    def __init__(self, buf, send_z, send_f, send_y, recv, place):
-        self.buf, self.send_z, self.send_f, self.send_y, self.recv = buf, send_z, send_f, send_y, recv
+class Spread:
+    def __init__(self, buf, send, recv, place):
+        self.buf, self.send, self.recv = buf, send, recv
         self.zl, self.y, self.tp, self.dp = place
-        self.me = self.zl * 4 + self.y
-        self.quad = (self.zl // 4) * 4
-        self.far = lax.rem(self.zl + 4, 8)
-        self.far_quad = 4 - self.quad
         self.sent = []
 
     def copy(self, block, sem, zl, y):
@@ -60,52 +56,27 @@
             device_id_type=MESH,
         )
 
-    def wait_block(self, block):
-        self.copy(block, self.send_z.at[0], self.far, self.y).wait_recv()
-
-    def near(self, d):
-        return self.quad + lax.rem(self.zl + d, 4)
-
-    def start(self, copy):
+    def wait(self, block):
+        self.copy(block, self.send.at[0], lax.rem(self.zl + 4, 8), self.y).wait_recv()
+
+    def start(self, block, zl, y):
+        copy = self.copy(block, self.send.at[len(self.sent)], zl, y)
         copy.start()
         self.sent.append(copy)
 
-    def spread_y(self, slot, block):
-        for d in (1, 3, 2):
-            self.start(self.copy(block, self.send_y.at[slot * 3 + d - 1], self.zl, lax.rem(self.y + d, 4)))
-
-    def first(self):
-        self.start(self.copy(self.me, self.send_z.at[0], self.far, self.y))
-        for d in (1, 2, 3):
-            self.start(self.copy(self.me, self.send_z.at[d], self.near(d), self.y))
-        self.spread_y(0, self.me)
-
-    def take_near(self):
-        for d in (1, 2, 3):
-            block = self.near(d) * 4 + self.y
-            self.wait_block(block)
-            self.spread_y(d, block)
-
-    def take_far(self):
-        block = self.far * 4 + self.y
-        self.wait_block(block)
-        for d in (1, 2, 3):
-            self.start(self.copy(block, self.send_f.at[d - 1], self.near(d), self.y))
-        self.spread_y(4, block)
-
-    def take_rest(self):
-        for d in (1, 2, 3):
-            block = (self.far_quad + lax.rem(self.zl + d, 4)) * 4 + self.y
-            self.wait_block(block)
-            self.spread_y(4 + d, block)
-
-    def take_y(self):
-        def layer(z, carry):
-            for d in (1, 2, 3):
-                self.wait_block(z * 4 + lax.rem(self.y + d, 4))
-            return carry
-
-        lax.fori_loop(0, 8, layer, 0)
+    def near(self, d):
+        return (self.zl // 4) * 4 + lax.rem(self.zl + d, 4)
+
+    def to_far(self, block):
+        self.start(block, lax.rem(self.zl + 4, 8), self.y)
+
+    def to_near(self, block):
+        for d in (2, 1, 3):
+            self.start(block, self.near(d), self.y)
+
+    def to_y(self, block):
+        for d in (2, 1, 3):
+            self.start(block, self.zl, lax.rem(self.y + d, 4))
 
     def finish(self):
         for copy in self.sent:
@@ -113,12 +84,12 @@
 
 
 def kernel(
-    qkv, resid, out_w, gain, bias, kv_w_hbm, host, pos, docs, text, queries,
+    qkv_hbm, resid_hbm, out_w_hbm, gain_hbm, bias_hbm, kv_w_hbm, host_hbm, pos_hbm, docs_hbm, text, queries_hbm,
     out,
-    kv_w, ctx, mine, stat, part_send, part_recv, part_own, pair_send, pair_recv, perm,
-    tbuf, vbuf, text_pos, frame_pos, m_s, l_s, acc_s,
+    qkv, resid, out_w, gain, bias, kv_w, host, pos, docs, queries, ctx, mine, stat, part_send, part_recv, part_own, pair_send, pair_recv, perm,
+    raw, tbuf, vbuf, text_pos, frame_pos, qt, m_s, l_s, acc_s,
     load_sem, cz_s, cz_r, cx_s, cx_r, cf_s, cf_r, st_s, st_r, rx_s, rx_r, rz_s, rz_r,
-    tz_s, tf_s, ty_s, t_r, vz_s, vf_s, vy_s, v_r,
+    raw_s, raw_r, t_s, t_r, v_s, v_r,
 ):
     c = lax.axis_index("ctx")
     tp = lax.axis_index("tp")
@@ -141,13 +112,21 @@
     for d in range(1, 4):
         pl.semaphore_signal(barrier, inc=1, device_id=(zl * 4 + lax.rem(y + d, 4), tp, dp), device_id_type=MESH)
 
-    load = pltpu.make_async_copy(kv_w_hbm, kv_w, load_sem.at[0])
-    load.start()
-    load_text = pltpu.make_async_copy(text, tbuf.at[c], load_sem.at[1])
-    load_text.start()
-
-    texts = Gather(tbuf, tz_s, tf_s, ty_s, t_r, (zl, y, tp, dp))
-    frames = Gather(vbuf, vz_s, vf_s, vy_s, v_r, (zl, y, tp, dp))
+    loads = []
+    for source, target in (
+        (qkv_hbm, qkv), (text, raw.at[zl // 4]), (pos_hbm, pos), (host_hbm, host), (docs_hbm, docs), (gain_hbm, gain),
+        (bias_hbm, bias), (out_w_hbm, out_w), (resid_hbm, resid), (queries_hbm, queries), (kv_w_hbm, kv_w),
+    ):
+        loads.append(pltpu.make_async_copy(source, target, load_sem.at[len(loads)]))
+        loads[-1].start()
+    load_qkv, load_text, *load_rest, load_kv_w = loads
+
+    place = (zl, y, tp, dp)
+    texts = Spread(tbuf, t_s, t_r, place)
+    frames = Spread(vbuf, v_s, v_r, place)
+    pair = lax.rem(c, 16)
+    quarter = lax.rem(zl, 4)
+    load_qkv.wait()
 
     keys = dot_nt(eye(FP, FP, BF16), qkv[1]).astype(BF16)
     sent = []
@@ -181,13 +160,27 @@
         for d in (1, 3, 2):
             begin(ctx_copy(tp, h, cx_s.at[h * 3 + d - 1], cx_r.at[h * 3 + d - 1], at_tp(zh, x_of(d))))
 
+    raw_copy = pltpu.make_async_remote_copy(
+        src_ref=raw.at[zl // 4],
+        dst_ref=raw.at[zl // 4],
+        send_sem=raw_s.at[0],
+        recv_sem=raw_r.at[0],
+        device_id=(lax.rem(c + 16, CTX), tp, dp),
+        device_id_type=MESH,
+    )
     load_text.wait()
-    texts.first()
-
-    slot = lax.broadcasted_iota(jnp.int32, (64, 32), 0) * FT
-    held = jnp.max(jnp.where(slot == pos[...], 1, 0), axis=1, keepdims=True)
-    slot_col = lax.broadcasted_iota(jnp.int32, (64, 1), 0) * FT
-    text_pos[...] = jnp.broadcast_to(jnp.where(held > 0, -1 << 20, slot_col), (64, 128))
+    for load in load_rest:
+        load.wait()
+
+    def slot_of(i):
+        return FT * (2 * lax.broadcasted_iota(jnp.int32, (16, 32), 0) + (0, 1, 32, 33)[i])
+
+    is_text = [jnp.max(jnp.where(slot_of(i) == pos[...], 1, 0), axis=1, keepdims=True) == 0 for i in range(4)]
+    slots = [slot_of(i)[:, :1] for i in range(4)]
+    early = jnp.where(is_text[0], slots[0], jnp.where(is_text[1], slots[1], slots[2]))
+    late = jnp.where(is_text[3], slots[3], jnp.where(is_text[2], slots[2], slots[1]))
+    text_pos[0] = jnp.broadcast_to(early, (16, 128))
+    text_pos[1] = jnp.broadcast_to(late, (16, 128))
     owner = lax.broadcasted_iota(jnp.int32, (CTX, 32), 0)
     frame_col = jnp.sum(jnp.where(owner == host[...], pos[...], 0), axis=1, keepdims=True)
     frame_pos[...] = jnp.broadcast_to(frame_col, (CTX, 128))
@@ -196,42 +189,54 @@
     for d in (1, 2, 3):
         before = jnp.sum(jnp.where(docs[...] < d, 1, 0), axis=(0, 1), keepdims=True)
         first = jnp.where(doc == d, before, first)
-    query_pos = c * T + lax.broadcasted_iota(jnp.int32, (1, T), 1)
+    first = jnp.concatenate([first] * GROUP, axis=1)
+    query_pos = c * T + lax.rem(lax.broadcasted_iota(jnp.int32, (1, GROUP * T), 1), T)
     m_s[...] = jnp.full(m_s.shape, NEGATIVE, F32)
     l_s[...] = jnp.zeros(l_s.shape, F32)
     acc_s[...] = jnp.zeros(acc_s.shape, F32)
-
-    def attend(kv, key_pos, causal):
-        k = kv[:, :HD]
-        vt = kv[:, HD:].T
-        allowed = key_pos >= first
-        if causal:
-            allowed = allowed & (key_pos <= query_pos)
-        for g in range(GROUP):
-            scores = dot_nt(k, queries[:, g * HD : (g + 1) * HD]) * (LOG2E / math.sqrt(HD))
-            scores = jnp.where(allowed, scores, NEGATIVE)
-            old = m_s[g : g + 1, :]
-            new = jnp.maximum(old, jnp.max(scores, axis=0, keepdims=True))
-            weights = jnp.exp2(scores - new)
-            factor = jnp.exp2(old - new)
-            m_s[g : g + 1, :] = new
-            l_s[g : g + 1, :] = l_s[g : g + 1, :] * factor + jnp.sum(weights, axis=0, keepdims=True)
-            acc_s[g] = acc_s[g] * factor + dot_nn(vt, weights.astype(BF16))
-
-    within = lax.broadcasted_iota(jnp.int32, (FT, T), 0)
-
-    def two(a, b):
-        return jnp.concatenate([within + jnp.concatenate([a, a], axis=1), within + jnp.concatenate([b, b], axis=1)], axis=0)
-
-    def text_block(b, causal):
-        attend(tbuf[b], two(text_pos[pl.ds(2 * b, 1), :], text_pos[pl.ds(2 * b + 1, 1), :]), causal)
-
-    def text_range(lo, hi):
-        def step(b, carry):
-            text_block(b, False)
-            return carry
-
-        lax.fori_loop(lo, hi, step, 0)
+    for g in range(GROUP):
+        qt[:, g * T : (g + 1) * T] = dot_nt(eye(HD, HD, BF16), queries[:, g * HD : (g + 1) * HD]).astype(BF16)
+
+    def attend(blocks, starts):
+        within = lax.broadcasted_iota(jnp.int32, (FT, GROUP * T), 0)
+        k = jnp.concatenate([b[:, :HD] for b in blocks], axis=0)
+        vt = jnp.concatenate([b[:, HD:] for b in blocks], axis=1)
+        key_pos = jnp.concatenate([within + jnp.concatenate([start] * 8, axis=1) for start in starts], axis=0)
+        scores = dot_nn(k, qt[...]) * (LOG2E / math.sqrt(HD))
+        scores = jnp.where((key_pos >= first) & (key_pos <= query_pos), scores, NEGATIVE)
+        old = m_s[...]
+        new = jnp.maximum(old, jnp.max(scores, axis=0, keepdims=True))
+        weights = jnp.exp2(scores - new)
+        factor = jnp.exp2(old - new)
+        m_s[...] = new
+        l_s[...] = l_s[...] * factor + jnp.sum(weights, axis=0, keepdims=True)
+        acc_s[...] = acc_s[...] * factor + dot_nn(vt, weights.astype(BF16))
+
+    def text_step(j, carry):
+        layer = lax.rem(quarter + j, 4)
+        for d in (1, 2, 3):
+            texts.wait(layer * 4 + lax.rem(y + d, 4))
+
+        @pl.when(layer <= zl)
+        def _():
+            held = [4 * layer + i for i in range(4)]
+            blocks = [tbuf[h, i * FT : (i + 1) * FT] for h in held for i in range(2)]
+            attend(blocks, [text_pos[i, pl.ds(h, 1), :] for h in held for i in range(2)])
+
+        return carry
+
+    def frame_step(j, carry):
+        layer = lax.rem(quarter + j, 4)
+        for far in range(2):
+            for d in (1, 2, 3):
+                frames.wait((layer + 4 * far) * 4 + lax.rem(y + d, 4))
+
+        @pl.when(layer <= zl)
+        def _():
+            held = [4 * layer + i + 16 * far for far in range(2) for i in range(4)]
+            attend([vbuf[h] for h in held], [frame_pos[pl.ds(h, 1), :] for h in held])
+
+        return carry
 
     r = lax.broadcasted_iota(jnp.int32, (FP, FP), 0)
     p = lax.broadcasted_iota(jnp.int32, (FP, FP), 1)
@@ -239,12 +244,11 @@
     gain_col = jnp.sum(jnp.where(eye(LOCAL, LOCAL, F32) > 0, gain[...], 0.0), axis=1, keepdims=True)
     bias_col = jnp.sum(jnp.where(eye(LOCAL, LOCAL, F32) > 0, bias[...], 0.0), axis=1, keepdims=True)
 
-    texts.take_near()
     for h in range(2):
         ctx_copy(other * 4 + x, h, cz_s.at[h], cz_r.at[h], at_tp(other, x)).wait_recv()
         for d in (1, 3, 2):
             begin(ctx_copy(other * 4 + x, h, cf_s.at[h * 3 + d - 1], cf_r.at[h * 3 + d - 1], at_tp(zh, x_of(d))))
-    texts.take_far()
+    begin(raw_copy)
     for h in range(2):
         for d in (1, 2, 3):
             ctx_copy(zh * 4 + x_of(4 - d), h, cx_s.at[0], cx_r.at[h * 3 + d - 1], at_tp(zh, x_of(d))).wait_recv()
@@ -274,7 +278,18 @@
 
     for d in range(1, TP):
         begin(stat_copy(tp, d, lax.rem(tp + d, TP)))
-    texts.take_rest()
+    raw_copy.wait_recv()
+    four = [raw[i, j * FT : (j + 1) * FT, :].astype(F32) for i in range(2) for j in range(2)]
+    for which in range(2):
+        start = text_pos[which, pl.ds(pair, 1), :]
+        start = jnp.concatenate([start, start], axis=1)
+        chosen = four[3]
+        for i in range(3):
+            chosen = jnp.where(start == FT * (2 * pair + (0, 1, 32)[i]), four[i], chosen)
+        tbuf[pair, which * FT : (which + 1) * FT, :HD] = chosen[:, :HD].astype(BF16)
+        tbuf[pair, which * FT : (which + 1) * FT, HD:] = chosen[:, HD:].T.astype(BF16)
+    texts.to_near(pair)
+    texts.to_y(pair)
     for d in range(1, TP):
         stat_copy(lax.rem(tp + TP - d, TP), d, lax.rem(tp + d, TP)).wait_recv()
     all_stats = stat[0]
@@ -287,7 +302,7 @@
     normed = ((mine[...] - mean_row) * scale_row * gain_col + bias_col).astype(BF16)
     grouped = dot_nt(perm[...], normed).astype(BF16)
 
-    load.wait()
+    load_kv_w.wait()
 
     def partial_kv(t):
         cols = pl.ds(pl.multiple_of(t * 2 * HD, 128), 2 * HD)
@@ -312,6 +327,10 @@
         begin(part_copy(d))
     part_own[0] = partial_kv(other * 4 + x)
     part_own[1] = partial_kv(zh * 4 + x)
+    for d in (2, 1, 3):
+        block = lax.rem(quarter + d, 4) * 4 + y
+        texts.wait(block)
+        texts.to_y(block)
     for d in (1, 2, 3):
         part_copy(d).wait_recv()
 
@@ -322,7 +341,7 @@
         return total
 
     pair_send[...] = summed(0, other).astype(BF16)
-    pair = pltpu.make_async_remote_copy(
+    last = pltpu.make_async_remote_copy(
         src_ref=pair_send,
         dst_ref=pair_recv,
         send_sem=rz_s.at[0],
@@ -330,31 +349,35 @@
         device_id=at_tp(other, x),
         device_id_type=MESH,
     )
-    begin(pair)
+    begin(last)
     part_own[1] = summed(1, zh)
-
-    texts.take_y()
-    middle = c // 2
-    text_range(0, middle)
-    pair.wait_recv()
-    vbuf[c] = (part_own[1] + pair_recv[...].astype(F32)).astype(BF16)
-    frames.first()
-    text_range(middle, c)
-    text_block(c, True)
-    frames.take_near()
-    frames.take_far()
-    frames.take_rest()
-    frames.take_y()
-
-    def frame_step(i, carry):
-        kv = jnp.concatenate([vbuf[i], vbuf[i + 16]], axis=0)
-        attend(kv, two(frame_pos[pl.ds(i, 1), :], frame_pos[pl.ds(i + 16, 1), :]), True)
-        return carry
-
-    lax.fori_loop(0, jnp.minimum(c, 15) + 1, frame_step, 0)
+    text_step(0, 0)
+    last.wait_recv()
+    own_kv = part_own[1] + pair_recv[...].astype(F32)
+    vbuf[c, :, :HD] = own_kv[:, :HD].astype(BF16)
+    vbuf[c, :, HD:] = own_kv[:, HD:].T.astype(BF16)
+    frames.to_far(c)
+    frames.to_near(c)
+    frames.to_y(c)
+    lax.fori_loop(1, 3, text_step, 0)
+    far = lax.rem(c + 16, CTX)
+    frames.wait(far)
+    frames.to_near(far)
+    frames.to_y(far)
+    for d in (2, 1, 3):
+        block = frames.near(d) * 4 + y
+        frames.wait(block)
+        frames.to_y(block)
+    for d in (2, 1, 3):
+        block = lax.rem(frames.near(d) + 4, 8) * 4 + y
+        frames.wait(block)
+        frames.to_y(block)
+    lax.fori_loop(3, 4, text_step, 0)
+    lax.fori_loop(0, 4, frame_step, 0)
 
     for g in range(GROUP):
-        result = (acc_s[g] / l_s[g : g + 1, :]).astype(BF16)
+        cols = slice(g * T, (g + 1) * T)
+        result = (acc_s[:, cols] / l_s[:, cols]).astype(BF16)
         out[:, g * HD : (g + 1) * HD] = dot_nt(eye(T, T, BF16), result).astype(BF16)
     for copy in sent:
         copy.wait_send()
@@ -371,10 +394,19 @@
     return pl.pallas_call(
         kernel,
         out_shape=jax.ShapeDtypeStruct((T, GROUP * HD), BF16),
-        in_specs=[vmem, vmem, vmem, vmem, vmem, hbm, vmem, vmem, vmem, hbm, vmem],
+        in_specs=[hbm] * 11,
         out_specs=vmem,
         scratch_shapes=[
+            pltpu.VMEM((3, LOCAL, FP), BF16),
+            pltpu.VMEM((LOCAL, FP), BF16),
+            pltpu.VMEM((LOCAL, VD), BF16),
+            pltpu.VMEM((1, LOCAL), F32),
+            pltpu.VMEM((1, LOCAL), F32),
             pltpu.VMEM((4, LOCAL, 8 * 2 * HD), BF16),
+            pltpu.VMEM((1, 32), jnp.int32),
+            pltpu.VMEM((1, 32), jnp.int32),
+            pltpu.VMEM((64, 128), jnp.int32),
+            pltpu.VMEM((T, GROUP * HD), BF16),
             pltpu.VMEM((VD, FP), BF16),
             pltpu.VMEM((LOCAL, FP), F32),
             pltpu.VMEM((TP, 8, 128), F32),
@@ -384,17 +416,19 @@
             pltpu.VMEM((FT, 2 * HD), BF16),
             pltpu.VMEM((FT, 2 * HD), BF16),
             pltpu.VMEM((FP, FP), BF16),
-            pltpu.VMEM((CTX, T, 2 * HD), BF16),
+            pltpu.VMEM((2, T, 2 * HD), BF16),
+            pltpu.VMEM((16, T, 2 * HD), BF16),
             pltpu.VMEM((CTX, FT, 2 * HD), BF16),
-            pltpu.VMEM((64, 128), jnp.int32),
+            pltpu.VMEM((2, 16, 128), jnp.int32),
             pltpu.VMEM((CTX, 128), jnp.int32),
-            pltpu.VMEM((8, T), F32),
-            pltpu.VMEM((8, T), F32),
-            pltpu.VMEM((GROUP, HD, T), F32),
-            dma(2), dma(2), dma(2), dma(6), dma(6), dma(6), dma(6), dma(7), dma(7), dma(3), dma(3), dma(1), dma(1),
-            dma(4), dma(3), dma(24), dma(CTX), dma(4), dma(3), dma(24), dma(CTX),
+            pltpu.VMEM((HD, GROUP * T), BF16),
+            pltpu.VMEM((1, GROUP * T), F32),
+            pltpu.VMEM((1, GROUP * T), F32),
+            pltpu.VMEM((HD, GROUP * T), F32),
+            dma(11), dma(2), dma(2), dma(6), dma(6), dma(6), dma(6), dma(7), dma(7), dma(3), dma(3), dma(1), dma(1),
+            dma(1), dma(1), dma(15), dma(16), dma(31), dma(CTX),
         ],
-        compiler_params=pltpu.CompilerParams(collective_id=0, has_side_effects=True, vmem_limit_bytes=48 * 2**20),
+        compiler_params=pltpu.CompilerParams(collective_id=0, has_side_effects=True, vmem_limit_bytes=60 * 2**20),
         name="window",
     )(
         jnp.transpose(vis_qkv, (1, 2, 0)),

time: 178 us -> 111 us (0.62)
  the two profiles are of different devices: /device:TPU:232 before, /device:TPU:33 now
where the time goes in v2:
time: 111 us; the launch traced here: 110 us
  Pallas kernels  107 us (96%)
  local copies, waits for them, and re-layouts  3.25 us (3%)
    pallas_call x1, Pallas kernels, shards(): pl.pallas_call(kernel, out_shape=jax.ShapeDtypeStruct((T, GROUP * HD), BF...  107 us
    unnamed x2, local copies, waits for them, and re-layouts  3.25 us

profile of v2, /device:TPU:33, one launch (start us, length us, event | category | flops | bytes accessed | tf_op | source)
XLA Modules:
  0.0 110.4 jit_solution(11343277717149396950)
XLA Ops:
  0.0 1.6 %copy.14 = bf16[32,8,2,128]{3,1,2,0:T(8,128)(2,1)} copy(bf16[32,8,2,128]{3,2,1,0:T(2,128)(2,1)} %bitcast.17) | data formatting | bytes 262144
  1.6 107.1 %window.1 = bf16[256,512]{1,0:T(8,128)(2,1)} custom-call(bf16[3,160,512]{2,1,0:T(8,128)(2,1)} %bitcast.14, bf16[160,512]{1,0:T(8,128)(2,1)} %bitcast.16, bf16[160,1280]{1,0:T(8,128)(2,1)} %bitcast.15, f32[1,160]{1,0:T(1,128)} %bitcast.19, f32[1,160]{1,0:T(1,128)} %bitcast.20, bf16[4,160,2048]{2,1,0:T(8,128)(2,1)} %kv_w_hbm.1, s32[1,32]{1,0:T(1,128)} %bitcast.21, ...), custom_call_target="tpu_custom_call" | custom-call | tf_op jit(solution)/shard_map/window/pallas_call | solution.py:394
  108.7 1.7 %copy.16 = bf16[256,512]{1,0:T(8,128)(2,1)} copy(bf16[256,512]{1,0:T(8,128)(2,1)} %window.1) | data formatting | bytes 524288

commit v3 on v2

v3 whole, which is shorter than its diff:
```python
import functools
import math

import jax
import jax.numpy as jnp
from jax import lax
from jax.experimental import pallas as pl
from jax.experimental.pallas import tpu as pltpu
from jax.sharding import PartitionSpec as P

VD = 1280
VH = 16
HD = 128
FT = 128
FP = 512
T = 256
GROUP = 4
LOCAL = 160
HEAD = 80
CTX = 32
TP = 8
PARTS = 2
WIDTH = FP // PARTS
TOKENS = FT // PARTS
NEGATIVE = -1e30
LOG2E = math.log2(math.e)
MESH = pl.DeviceIdType.MESH
F32 = jnp.float32
BF16 = jnp.bfloat16


def dot_nt(a, b):
    return lax.dot_general(a, b, (((1,), (1,)), ((), ())), preferred_element_type=F32)


def dot_nn(a, b):
    return lax.dot_general(a, b, (((1,), (0,)), ((), ())), preferred_element_type=F32)


def eye(rows, cols, dtype):
    r = lax.broadcasted_iota(jnp.int32, (rows, cols), 0)
    c = lax.broadcasted_iota(jnp.int32, (rows, cols), 1)
    return jnp.where(r == c, 1.0, 0.0).astype(dtype)


class Spread:
    def __init__(self, buf, send, recv, place):
        self.buf, self.send, self.recv = buf, send, recv
        self.zl, self.y, self.tp, self.dp = place
        self.sent = []

    def copy(self, block, sem, zl, y):
        return pltpu.make_async_remote_copy(
            src_ref=self.buf.at[block],
            dst_ref=self.buf.at[block],
            send_sem=sem,
            recv_sem=self.recv.at[block],
            device_id=(zl * 4 + y, self.tp, self.dp),
            device_id_type=MESH,
        )

    def wait(self, block):
        self.copy(block, self.send.at[0], lax.rem(self.zl + 4, 8), self.y).wait_recv()

    def start(self, block, zl, y):
        copy = self.copy(block, self.send.at[len(self.sent)], zl, y)
        copy.start()
        self.sent.append(copy)

    def near(self, d):
        return (self.zl // 4) * 4 + lax.rem(self.zl + d, 4)

    def to_far(self, block):
        self.start(block, lax.rem(self.zl + 4, 8), self.y)

    def to_near(self, block):
        for d in (2, 3, 1):
            self.start(block, self.near(d), self.y)

    def to_y(self, block):
        for d in (2, 1, 3):
            self.start(block, self.zl, lax.rem(self.y + d, 4))

    def finish(self):
        for copy in self.sent:
            copy.wait_send()


def kernel(
    qkv_hbm, resid_hbm, out_w_hbm, gain_hbm, bias_hbm, kv_w_hbm, host_hbm, pos_hbm, docs_hbm, text, queries_hbm,
    out,
    qkv, resid, out_w, gain, bias, kv_w, host, pos, docs, queries, ctx, mine, stat, part_send, part_recv, part_own, pair_send, pair_recv, perm,
    raw, tbuf, vbuf, text_pos, frame_pos, qt, m_s, l_s, acc_s,
    load_sem, cz_s, cz_r, cx_s, cx_r, cf_s, cf_r, st_s, st_r, rx_s, rx_r, rz_s, rz_r,
    known, raw_s, raw_r, t_s, t_r, v_s, v_r,
):
    c = lax.axis_index("ctx")
    tp = lax.axis_index("tp")
    dp = lax.axis_index("dp")
    zl, y = c // 4, lax.rem(c, 4)
    zh, x = tp // 4, lax.rem(tp, 4)
    other = 1 - zh

    def at_tp(h, col):
        return (c, h * 4 + col, dp)

    def x_of(d):
        return lax.rem(x + d, 4)

    def along_z(d):
        z = lax.rem(zh * 8 + zl + d, 16)
        return (lax.rem(z, 8) * 4 + y, (z // 8) * 4 + x, dp)

    barrier = pltpu.get_barrier_semaphore()
    contacts = [along_z(4), along_z(12)]
    for d in (1, 2, 3):
        contacts.append(at_tp(zh, x_of(d)))
        contacts.append((zl * 4 + lax.rem(y + d, 4), tp, dp))
        contacts.append((((zl // 4) * 4 + lax.rem(zl + d, 4)) * 4 + y, tp, dp))
    for contact in contacts:
        pl.semaphore_signal(barrier, inc=1, device_id=contact, device_id_type=MESH)

    loads = []
    for source, target in (
        (qkv_hbm, qkv), (text, raw.at[zl // 4]), (pos_hbm, pos), (host_hbm, host), (docs_hbm, docs), (gain_hbm, gain),
        (bias_hbm, bias), (out_w_hbm, out_w), (resid_hbm, resid), (queries_hbm, queries), (kv_w_hbm, kv_w),
    ):
        loads.append(pltpu.make_async_copy(source, target, load_sem.at[len(loads)]))
        loads[-1].start()
    load_qkv, load_text, *load_rest, load_kv_w = loads

    place = (zl, y, tp, dp)
    texts = Spread(tbuf, t_s, t_r, place)
    frames = [Spread(vbuf.at[a], v_s.at[a], v_r.at[a], place) for a in range(PARTS)]
    pair = lax.rem(c, 16)
    quarter = lax.rem(zl, 4)
    load_qkv.wait()

    keys = dot_nt(eye(FP, FP, BF16), qkv[1]).astype(BF16)
    sent = []

    def ctx_copy(a, t, send, recv, target):
        rows = pl.ds(pl.multiple_of(t * LOCAL, 16), LOCAL)
        return pltpu.make_async_remote_copy(
            src_ref=ctx.at[a, rows],
            dst_ref=ctx.at[a, rows],
            send_sem=send,
            recv_sem=recv,
            device_id=target,
            device_id_type=MESH,
        )

    def begin(copy):
        copy.start()
        sent.append(copy)

    raw_copy = pltpu.make_async_remote_copy(
        src_ref=raw.at[zl // 4],
        dst_ref=raw.at[zl // 4],
        send_sem=raw_s.at[0],
        recv_sem=raw_r.at[0],
        device_id=(lax.rem(c + 16, CTX), tp, dp),
        device_id_type=MESH,
    )
    for h in range(2):
        head = slice(h * HEAD, (h + 1) * HEAD)
        scores = dot_nn(keys[:, head], qkv[0, head, :]) * (LOG2E / math.sqrt(HEAD))
        top = jnp.max(scores, axis=0, keepdims=True)
        weights = jnp.exp2(scores - top)
        total = jnp.sum(weights, axis=0, keepdims=True)
        mixed = (dot_nn(qkv[2, head, :], weights.astype(BF16)) / total).astype(BF16)
        for a in range(PARTS):
            ctx[a, pl.ds(pl.multiple_of(tp * LOCAL + h * HEAD, 16), HEAD), :] = mixed[:, a * WIDTH : (a + 1) * WIDTH]
        if h == 0:
            pl.semaphore_wait(barrier, len(contacts))
            for i, d in enumerate((4, 12)):
                pl.semaphore_signal(known.at[i], inc=1, device_id=along_z(d), device_id_type=MESH)
    load_text.wait()
    pl.semaphore_wait(known.at[0], 1)
    pl.semaphore_wait(known.at[1], 1)
    for a in range(PARTS):
        begin(ctx_copy(a, tp, cz_s.at[a], cz_r.at[a], at_tp(other, x)))
    for a in range(PARTS):
        for d in (2, 1, 3):
            begin(ctx_copy(a, tp, cx_s.at[a * 3 + d - 1], cx_r.at[a * 3 + d - 1], at_tp(zh, x_of(d))))

    for load in load_rest:
        load.wait()

    def slot_of(i):
        return FT * (2 * lax.broadcasted_iota(jnp.int32, (16, 32), 0) + (0, 1, 32, 33)[i])

    is_text = [jnp.max(jnp.where(slot_of(i) == pos[...], 1, 0), axis=1, keepdims=True) == 0 for i in range(4)]
    slots = [slot_of(i)[:, :1] for i in range(4)]
    early = jnp.where(is_text[0], slots[0], jnp.where(is_text[1], slots[1], slots[2]))
    late = jnp.where(is_text[3], slots[3], jnp.where(is_text[2], slots[2], slots[1]))
    text_pos[0] = jnp.broadcast_to(early, (16, 128))
    text_pos[1] = jnp.broadcast_to(late, (16, 128))
    owner = lax.broadcasted_iota(jnp.int32, (CTX, 32), 0)
    frame_col = jnp.sum(jnp.where(owner == host[...], pos[...], 0), axis=1, keepdims=True)
    frame_pos[...] = jnp.broadcast_to(frame_col, (CTX, 128))
    doc = jnp.concatenate([docs[pl.ds(2 * c, 1), :], docs[pl.ds(2 * c + 1, 1), :]], axis=1)
    first = jnp.zeros((1, T), jnp.int32)
    for d in (1, 2, 3):
        before = jnp.sum(jnp.where(docs[...] < d, 1, 0), axis=(0, 1), keepdims=True)
        first = jnp.where(doc == d, before, first)
    first = jnp.concatenate([first] * GROUP, axis=1)
    query_pos = c * T + lax.rem(lax.broadcasted_iota(jnp.int32, (1, GROUP * T), 1), T)
    m_s[...] = jnp.full(m_s.shape, NEGATIVE, F32)
    l_s[...] = jnp.zeros(l_s.shape, F32)
    acc_s[...] = jnp.zeros(acc_s.shape, F32)
    for g in range(GROUP):
        qt[:, g * T : (g + 1) * T] = dot_nt(eye(HD, HD, BF16), queries[:, g * HD : (g + 1) * HD]).astype(BF16)

    def attend(k, vt, starts):
        within = lax.broadcasted_iota(jnp.int32, (k.shape[0] // len(starts), GROUP * T), 0)
        key_pos = jnp.concatenate([within + jnp.concatenate([start] * 8, axis=1) for start in starts], axis=0)
        scores = dot_nn(k, qt[...]) * (LOG2E / math.sqrt(HD))
        scores = jnp.where((key_pos >= first) & (key_pos <= query_pos), scores, NEGATIVE)
        old = m_s[...]
        new = jnp.maximum(old, jnp.max(scores, axis=0, keepdims=True))
        weights = jnp.exp2(scores - new)
        factor = jnp.exp2(old - new)
        m_s[...] = new
        l_s[...] = l_s[...] * factor + jnp.sum(weights, axis=0, keepdims=True)
        acc_s[...] = acc_s[...] * factor + dot_nn(vt, weights.astype(BF16))

    def text_step(j, carry):
        layer = lax.rem(quarter + j, 4)
        for d in (1, 2, 3):
            texts.wait(layer * 4 + lax.rem(y + d, 4))

        @pl.when(layer <= zl)
        def _():
            held = [4 * layer + i for i in range(4)]
            blocks = [tbuf[h, i * FT : (i + 1) * FT] for h in held for i in range(2)]
            k = jnp.concatenate([b[:, :HD] for b in blocks], axis=0)
            vt = jnp.concatenate([b[:, HD:] for b in blocks], axis=1)
            attend(k, vt, [text_pos[i, pl.ds(h, 1), :] for h in held for i in range(2)])

        return carry

    def frame_step(a, j):
        layer = lax.rem(quarter + j, 4)
        for far in range(2):
            for d in (1, 2, 3):
                frames[a].wait((layer + 4 * far) * 4 + lax.rem(y + d, 4))

        @pl.when(layer <= zl)
        def _():
            held = [4 * layer + i + 16 * far for far in range(2) for i in range(4)]
            k = jnp.concatenate([vbuf[a, h, :, :HD] for h in held], axis=0)
            v = jnp.concatenate([vbuf[a, h, :, HD:] for h in held], axis=0)
            attend(k, v.T, [frame_pos[pl.ds(h, 1), :] + a * TOKENS for h in held])

    r = lax.broadcasted_iota(jnp.int32, (WIDTH, WIDTH), 0)
    p = lax.broadcasted_iota(jnp.int32, (WIDTH, WIDTH), 1)
    perm[...] = jnp.where((r % TOKENS) * 4 + r // TOKENS == p, 1.0, 0.0).astype(BF16)
    gain_col = jnp.sum(jnp.where(eye(LOCAL, LOCAL, F32) > 0, gain[...], 0.0), axis=1, keepdims=True)
    bias_col = jnp.sum(jnp.where(eye(LOCAL, LOCAL, F32) > 0, bias[...], 0.0), axis=1, keepdims=True)

    def compact():
        raw_copy.wait_recv()
        four = [raw[i, j * FT : (j + 1) * FT, :].astype(F32) for i in range(2) for j in range(2)]
        for which in range(2):
            start = text_pos[which, pl.ds(pair, 1), :]
            start = jnp.concatenate([start, start], axis=1)
            chosen = four[3]
            for i in range(3):
                chosen = jnp.where(start == FT * (2 * pair + (0, 1, 32)[i]), four[i], chosen)
            tbuf[pair, which * FT : (which + 1) * FT, :HD] = chosen[:, :HD].astype(BF16)
            tbuf[pair, which * FT : (which + 1) * FT, HD:] = chosen[:, HD:].T.astype(BF16)
        texts.to_near(pair)
        texts.to_y(pair)

    for a in range(PARTS):
        ctx_copy(a, other * 4 + x, cz_s.at[a], cz_r.at[a], at_tp(other, x)).wait_recv()
        for d in (2, 1, 3):
            begin(ctx_copy(a, other * 4 + x, cf_s.at[a * 3 + d - 1], cf_r.at[a * 3 + d - 1], at_tp(zh, x_of(d))))
        if a == 0:
            begin(raw_copy)
    half = lambda i: pl.ds(pl.multiple_of(i * (VD // 2), 128), VD // 2)

    def stat_copy(a, t, d, target):
        return pltpu.make_async_remote_copy(
            src_ref=stat.at[a, t],
            dst_ref=stat.at[a, t],
            send_sem=st_s.at[a * 7 + d - 1],
            recv_sem=st_r.at[a * 7 + d - 1],
            device_id=(c, target, dp),
            device_id_type=MESH,
        )

    lanes = WIDTH // 128
    for a in range(PARTS):
        for d in (1, 2, 3):
            ctx_copy(a, zh * 4 + x_of(4 - d), cx_s.at[0], cx_r.at[a * 3 + d - 1], at_tp(zh, x_of(d))).wait_recv()
        hidden = resid[:, a * WIDTH : (a + 1) * WIDTH].astype(F32) + dot_nn(out_w[:, half(zh)], ctx[a, half(zh), :])
        for d in (1, 2, 3):
            ctx_copy(a, other * 4 + x_of(4 - d), cf_s.at[0], cf_r.at[a * 3 + d - 1], at_tp(zh, x_of(d))).wait_recv()
        hidden = hidden + dot_nn(out_w[:, half(other)], ctx[a, half(other), :])
        mine[a] = hidden
        sums = jnp.sum(hidden, axis=0, keepdims=True)
        squares = jnp.sum(hidden * hidden, axis=0, keepdims=True)
        stat[a, tp] = jnp.zeros((8, 128), F32)
        for i in range(lanes):
            stat[a, tp, i : i + 1, :] = sums[:, i * 128 : (i + 1) * 128]
            stat[a, tp, 4 + i : 5 + i, :] = squares[:, i * 128 : (i + 1) * 128]
        for d in (6, 2, 4, 5, 3, 1, 7):
            begin(stat_copy(a, tp, d, lax.rem(tp + d, TP)))

    load_kv_w.wait()

    def part_copy(a, d):
        return pltpu.make_async_remote_copy(
            src_ref=part_send.at[a, d - 1],
            dst_ref=part_recv.at[a, d - 1],
            send_sem=rx_s.at[a * 3 + d - 1],
            recv_sem=rx_r.at[a * 3 + d - 1],
            device_id=at_tp(zh, x_of(d)),
            device_id_type=MESH,
        )

    for a in range(PARTS):
        for d in range(1, TP):
            stat_copy(a, lax.rem(tp + TP - d, TP), d, lax.rem(tp + d, TP)).wait_recv()
        all_stats = stat[a, 0]
        for t in range(1, TP):
            all_stats = all_stats + stat[a, t]
        mean = all_stats[0:4] * (1.0 / VD)
        scale = lax.rsqrt(all_stats[4:8] * (1.0 / VD) - mean * mean + 1e-6)
        mean_row = jnp.concatenate([mean[i : i + 1] for i in range(lanes)], axis=1)
        scale_row = jnp.concatenate([scale[i : i + 1] for i in range(lanes)], axis=1)
        normed = ((mine[a] - mean_row) * scale_row * gain_col + bias_col).astype(BF16)
        grouped = dot_nt(perm[...], normed).astype(BF16)

        def partial_kv(t):
            cols = pl.ds(pl.multiple_of(t * 2 * HD, 128), 2 * HD)
            total = dot_nn(grouped[:TOKENS], kv_w[0, :, cols])
            for j in range(1, 4):
                total = total + dot_nn(grouped[j * TOKENS : (j + 1) * TOKENS], kv_w[j, :, cols])
            return total

        for d in (2, 1, 3):
            for i in range(2):
                part_send[a, d - 1, i] = partial_kv(i * 4 + x_of(d)).astype(BF16)
            begin(part_copy(a, d))
        if a == 0:
            compact()
        part_own[a, 0] = partial_kv(other * 4 + x)
        part_own[a, 1] = partial_kv(zh * 4 + x)

    def summed(a, slot, which):
        total = part_own[a, slot]
        for d in range(3):
            total = total + part_recv[a, d, which].astype(F32)
        return total

    def pair_copy(a):
        return pltpu.make_async_remote_copy(
            src_ref=pair_send.at[a],
            dst_ref=pair_recv.at[a],
            send_sem=rz_s.at[a],
            recv_sem=rz_r.at[a],
            device_id=at_tp(other, x),
            device_id_type=MESH,
        )

    for a in range(PARTS):
        for d in (1, 2, 3):
            part_copy(a, d).wait_recv()
        pair_send[a] = summed(a, 0, other).astype(BF16)
        begin(pair_copy(a))
        part_own[a, 1] = summed(a, 1, zh)
    for d in (2, 1, 3):
        block = lax.rem(quarter + d, 4) * 4 + y
        texts.wait(block)
        texts.to_y(block)
    text_step(0, 0)
    far = lax.rem(c + 16, CTX)
    for a in range(PARTS):
        pair_copy(a).wait_recv()
        vbuf[a, c] = (part_own[a, 1] + pair_recv[a].astype(F32)).astype(BF16)
        frames[a].to_far(c)
        frames[a].to_near(c)
        frames[a].to_y(c)
    for a in range(PARTS):
        frames[a].wait(far)
        frames[a].to_near(far)
        frames[a].to_y(far)
        for d in (2, 1, 3):
            block = frames[a].near(d) * 4 + y
            frames[a].wait(block)
            frames[a].to_y(block)
    lax.fori_loop(1, 3, text_step, 0)
    for a in range(PARTS):
        for d in (2, 1, 3):
            block = lax.rem(frames[a].near(d) + 4, 8) * 4 + y
            frames[a].wait(block)
            frames[a].to_y(block)
    lax.fori_loop(3, 4, text_step, 0)
    for a in range(PARTS):

        def step(j, carry):
            frame_step(a, j)
            return carry

        lax.fori_loop(0, 4, step, 0)

    for g in range(GROUP):
        cols = slice(g * T, (g + 1) * T)
        result = (acc_s[:, cols] / l_s[:, cols]).astype(BF16)
        out[:, g * HD : (g + 1) * HD] = dot_nt(eye(T, T, BF16), result).astype(BF16)
    for copy in sent:
        copy.wait_send()
    texts.finish()
    for part in frames:
        part.finish()


def shards(
    vis_qkv, vis_resid, vis_out_w, merge_gain, merge_bias, vis_kv_w, frame_host, vis_pos, doc_ids, text_kv, queries
):
    vmem = pl.BlockSpec(memory_space=pltpu.VMEM)
    hbm = pl.BlockSpec(memory_space=pl.ANY)
    dma = lambda n: pltpu.SemaphoreType.DMA((n,))
    return pl.pallas_call(
        kernel,
        out_shape=jax.ShapeDtypeStruct((T, GROUP * HD), BF16),
        in_specs=[hbm] * 11,
        out_specs=vmem,
        scratch_shapes=[
            pltpu.VMEM((3, LOCAL, FP), BF16),
            pltpu.VMEM((LOCAL, FP), BF16),
            pltpu.VMEM((LOCAL, VD), BF16),
            pltpu.VMEM((1, LOCAL), F32),
            pltpu.VMEM((1, LOCAL), F32),
            pltpu.VMEM((4, LOCAL, 8 * 2 * HD), BF16),
            pltpu.VMEM((1, 32), jnp.int32),
            pltpu.VMEM((1, 32), jnp.int32),
            pltpu.VMEM((64, 128), jnp.int32),
            pltpu.VMEM((T, GROUP * HD), BF16),
            pltpu.VMEM((PARTS, VD, WIDTH), BF16),
            pltpu.VMEM((PARTS, LOCAL, WIDTH), F32),
            pltpu.VMEM((PARTS, TP, 8, 128), F32),
            pltpu.VMEM((PARTS, 3, 2, TOKENS, 2 * HD), BF16),
            pltpu.VMEM((PARTS, 3, 2, TOKENS, 2 * HD), BF16),
            pltpu.VMEM((PARTS, 2, TOKENS, 2 * HD), F32),
            pltpu.VMEM((PARTS, TOKENS, 2 * HD), BF16),
            pltpu.VMEM((PARTS, TOKENS, 2 * HD), BF16),
            pltpu.VMEM((WIDTH, WIDTH), BF16),
            pltpu.VMEM((2, T, 2 * HD), BF16),
            pltpu.VMEM((16, T, 2 * HD), BF16),
            pltpu.VMEM((PARTS, CTX, TOKENS, 2 * HD), BF16),
            pltpu.VMEM((2, 16, 128), jnp.int32),
            pltpu.VMEM((CTX, 128), jnp.int32),
            pltpu.VMEM((HD, GROUP * T), BF16),
            pltpu.VMEM((1, GROUP * T), F32),
            pltpu.VMEM((1, GROUP * T), F32),
            pltpu.VMEM((HD, GROUP * T), F32),
            dma(11), dma(PARTS), dma(PARTS), dma(3 * PARTS), dma(3 * PARTS), dma(3 * PARTS), dma(3 * PARTS),
            dma(7 * PARTS), dma(7 * PARTS), dma(3 * PARTS), dma(3 * PARTS), dma(PARTS), dma(PARTS),
            pltpu.SemaphoreType.REGULAR((2,)), dma(1), dma(1), dma(15), dma(16), pltpu.SemaphoreType.DMA((PARTS, 31)), pltpu.SemaphoreType.DMA((PARTS, CTX)),
        ],
        compiler_params=pltpu.CompilerParams(collective_id=0, has_side_effects=True, vmem_limit_bytes=60 * 2**20),
        name="window",
    )(
        jnp.transpose(vis_qkv, (1, 2, 0)),
        jnp.transpose(vis_resid),
        jnp.transpose(vis_out_w),
        merge_gain.reshape(1, LOCAL),
        merge_bias.reshape(1, LOCAL),
        vis_kv_w,
        frame_host.reshape(1, 32),
        vis_pos.reshape(1, 32),
        doc_ids.reshape(64, 128),
        text_kv.reshape(T, 2 * HD),
        queries,
    )


def solution(mesh):
    return jax.shard_map(
        shards,
        mesh=mesh,
        in_specs=(
            P(("dp", "ctx"), None, "tp"),
            P(("dp", "ctx"), "tp"),
            P(None, "tp"),
            P("tp"),
            P("tp"),
            P(None, "tp", None),
            P("dp"),
            P("dp"),
            P("dp"),
            P(("dp", "ctx"), "tp", None, None),
            P(("dp", "ctx"), "tp"),
        ),
        out_specs=P(("dp", "ctx"), "tp"),
        check_vma=False,
    )
```

time: 111 us -> 108 us (0.973)
  the two profiles are of different devices: /device:TPU:33 before, /device:TPU:96 now
where the time goes in v3:
time: 108 us
  Pallas kernels  104 us (96%)
  local copies, waits for them, and re-layouts  3.25 us (3%)
    pallas_call x1, Pallas kernels, shards(): pl.pallas_call(kernel, out_shape=jax.ShapeDtypeStruct((T, GROUP * HD), BF...  104 us
    unnamed x2, local copies, waits for them, and re-layouts  3.25 us

profile of v3, /device:TPU:96, one launch (start us, length us, event | category | flops | bytes accessed | tf_op | source)
XLA Modules:
  0.0 107.7 jit_solution(14440774553769424645)
XLA Ops:
  0.0 1.6 %copy.14 = bf16[32,8,2,128]{3,1,2,0:T(8,128)(2,1)} copy(bf16[32,8,2,128]{3,2,1,0:T(2,128)(2,1)} %bitcast.17) | data formatting | bytes 262144
  1.6 104.4 %window.1 = bf16[256,512]{1,0:T(8,128)(2,1)} custom-call(bf16[3,160,512]{2,1,0:T(8,128)(2,1)} %bitcast.14, bf16[160,512]{1,0:T(8,128)(2,1)} %bitcast.16, bf16[160,1280]{1,0:T(8,128)(2,1)} %bitcast.15, f32[1,160]{1,0:T(1,128)} %bitcast.19, f32[1,160]{1,0:T(1,128)} %bitcast.20, bf16[4,160,2048]{2,1,0:T(8,128)(2,1)} %kv_w_hbm.1, s32[1,32]{1,0:T(1,128)} %bitcast.21, ...), custom_call_target="tpu_custom_call" | custom-call | tf_op jit(solution)/shard_map/window/pallas_call | solution.py:427
  106.0 1.7 %copy.16 = bf16[256,512]{1,0:T(8,128)(2,1)} copy(bf16[256,512]{1,0:T(8,128)(2,1)} %window.1) | data formatting | bytes 524288

commit v4 on v3

--- a/solution.py
+++ b/solution.py
@@ -261,15 +261,15 @@
 
     def compact():
         raw_copy.wait_recv()
-        four = [raw[i, j * FT : (j + 1) * FT, :].astype(F32) for i in range(2) for j in range(2)]
+        four = [raw[i, j * FT : (j + 1) * FT].astype(F32) for i in range(2) for j in range(2)]
         for which in range(2):
             start = text_pos[which, pl.ds(pair, 1), :]
-            start = jnp.concatenate([start, start], axis=1)
+            start = start.reshape(1, 1, HD)
             chosen = four[3]
             for i in range(3):
                 chosen = jnp.where(start == FT * (2 * pair + (0, 1, 32)[i]), four[i], chosen)
-            tbuf[pair, which * FT : (which + 1) * FT, :HD] = chosen[:, :HD].astype(BF16)
-            tbuf[pair, which * FT : (which + 1) * FT, HD:] = chosen[:, HD:].T.astype(BF16)
+            tbuf[pair, which * FT : (which + 1) * FT, :HD] = chosen[:, 0, :].astype(BF16)
+            tbuf[pair, which * FT : (which + 1) * FT, HD:] = chosen[:, 1, :].T.astype(BF16)
         texts.to_near(pair)
         texts.to_y(pair)
 
@@ -449,7 +449,7 @@
             pltpu.VMEM((PARTS, TOKENS, 2 * HD), BF16),
             pltpu.VMEM((PARTS, TOKENS, 2 * HD), BF16),
             pltpu.VMEM((WIDTH, WIDTH), BF16),
-            pltpu.VMEM((2, T, 2 * HD), BF16),
+            pltpu.VMEM((2, T, 2, HD), BF16),
             pltpu.VMEM((16, T, 2 * HD), BF16),
             pltpu.VMEM((PARTS, CTX, TOKENS, 2 * HD), BF16),
             pltpu.VMEM((2, 16, 128), jnp.int32),
@@ -474,7 +474,7 @@
         frame_host.reshape(1, 32),
         vis_pos.reshape(1, 32),
         doc_ids.reshape(64, 128),
-        text_kv.reshape(T, 2 * HD),
+        text_kv.reshape(T, 2, HD),
         queries,
     )
 

time: 108 us -> 107 us (level)
  local copies, waits for them, and re-layouts: 3.25 us -> 1.67 us
    unnamed x2 -> x1, local copies, waits for them, and re-layouts: 3.25 us -> 1.67 us
where the time goes in v4:
time: 107 us
  Pallas kernels  105 us (98%)
  local copies, waits for them, and re-layouts  1.67 us (2%)
    pallas_call x1, Pallas kernels, shards(): pl.pallas_call(kernel, out_shape=jax.ShapeDtypeStruct((T, GROUP * HD), BF...  105 us

profile of v4, /device:TPU:96, one launch (start us, length us, event | category | flops | bytes accessed | tf_op | source)
XLA Modules:
  0.0 106.6 jit_solution(11372396420478390920)
XLA Ops:
  0.0 104.9 %window.1 = bf16[256,512]{1,0:T(8,128)(2,1)} custom-call(bf16[3,160,512]{2,1,0:T(8,128)(2,1)} %bitcast.9, bf16[160,512]{1,0:T(8,128)(2,1)} %bitcast.11, bf16[160,1280]{1,0:T(8,128)(2,1)} %bitcast.10, f32[1,160]{1,0:T(1,128)} %bitcast.14, f32[1,160]{1,0:T(1,128)} %bitcast.15, bf16[4,160,2048]{2,1,0:T(8,128)(2,1)} %kv_w_hbm.1, s32[1,32]{1,0:T(1,128)} %bitcast.16, ...), custom_call_target="tpu_custom_call" | custom-call | tf_op jit(solution)/shard_map/window/pallas_call | solution.py:427
  104.9 1.7 %copy.13 = bf16[256,512]{1,0:T(8,128)(2,1)} copy(bf16[256,512]{1,0:T(8,128)(2,1)} %window.1) | data formatting | bytes 524288

commit v5 on v4

--- a/solution.py
+++ b/solution.py
@@ -388,6 +388,7 @@
         frames[a].wait(far)
         frames[a].to_near(far)
         frames[a].to_y(far)
+    for a in range(PARTS):
         for d in (2, 1, 3):
             block = frames[a].near(d) * 4 + y
             frames[a].wait(block)

time: 107 us -> 107 us (level)
  no operation moved by 1% of the time
where the time goes in v5:
time: 107 us
  Pallas kernels  105 us (98%)
  local copies, waits for them, and re-layouts  1.67 us (2%)
    pallas_call x1, Pallas kernels, shards(): pl.pallas_call(kernel, out_shape=jax.ShapeDtypeStruct((T, GROUP * HD), BF...  105 us

profile of v5, /device:TPU:96, one launch (start us, length us, event | category | flops | bytes accessed | tf_op | source)
XLA Modules:
  0.0 106.6 jit_solution(8981202810679475089)
XLA Ops:
  0.0 104.9 %window.1 = bf16[256,512]{1,0:T(8,128)(2,1)} custom-call(bf16[3,160,512]{2,1,0:T(8,128)(2,1)} %bitcast.9, bf16[160,512]{1,0:T(8,128)(2,1)} %bitcast.11, bf16[160,1280]{1,0:T(8,128)(2,1)} %bitcast.10, f32[1,160]{1,0:T(1,128)} %bitcast.14, f32[1,160]{1,0:T(1,128)} %bitcast.15, bf16[4,160,2048]{2,1,0:T(8,128)(2,1)} %kv_w_hbm.1, s32[1,32]{1,0:T(1,128)} %bitcast.16, ...), custom_call_target="tpu_custom_call" | custom-call | tf_op jit(solution)/shard_map/window/pallas_call | solution.py:428
  104.9 1.7 %copy.13 = bf16[256,512]{1,0:T(8,128)(2,1)} copy(bf16[256,512]{1,0:T(8,128)(2,1)} %window.1) | data formatting | bytes 524288
